TPU v7x, 512 devices: a whole 4x4x16 slice. The times are simulated.
512 devices in a mesh: grp: 4 (over y), resp: 16 (over z_lo, core), tp: 8 (over z_hi, x).
Axes of the slice: x: 4, y: 4, z: 16 (z_hi: 2, z_lo: 8; z = z_hi * 8 + z_lo), core: 2. Of those that a mesh axis runs over, the one named last changes fastest.
Arguments:
- queries: bfloat16 [8192, 64, 576], P(('grp', 'resp'), 'tp'), parts along dimension 0, may hold values from -44 to 44
- grad_out: bfloat16 [8192, 64, 512], P(('grp', 'resp'), 'tp'), parts along dimension 0, may hold values from -32 to 32
- prompt_kv: bfloat16 [3072, 576], P(('grp', 'resp')), parts along dimension 0, may hold values from -5 to 5
- resp_kv: bfloat16 [8192, 576], P(('grp', 'resp')), parts along dimension 0, may hold values from -6 to 6
- lengths: int32 [64], P(('grp', 'resp')), parts along dimension 0, may hold values from 16 to 128, as said below
Outputs:
- grad_queries: bfloat16 [8192, 64, 576], P(('grp', 'resp'), 'tp'), parts along dimension 0
- grad_prompt: bfloat16 [3072, 576], P(('grp', 'resp')), parts along dimension 0
- grad_resp: bfloat16 [8192, 576], P(('grp', 'resp')), parts along dimension 0
There are 4 independent parts, one for each index of `grp`. A program takes and returns all parts, laid end to end along the dimension named above; each array names one. Nothing has to cross between parts.
Inputs may be any that keep to these rules, and one draw needn't show every extreme that they name: `lengths`: every response has length 16 or more, and some response has length 128.
All inputs are finite; a program needn't handle non-finite values.
Results may differ from a plain program's by a relative error of at most 0.012.
Values may be sent and summed in bfloat16 or wider, within the bound.
No kernel may reach another device: no remote copies, remote signals or barrier semaphores. Data moves between devices by JAX's collectives and lax.ppermute only.
A program may use at most 64 MiB of HBM per device.

v0:
```python
import jax
import jax.numpy as jnp
from jax import lax
from jax.sharding import PartitionSpec as P

softmax_scale = 192 ** (-0.5)
masked_value = -1e30


def local_grads(queries, grad_out, prompt_all, resp_kv, length):
    rows, heads, width = queries.shape
    latent = grad_out.shape[2]
    prompt_rows = prompt_all.shape[0]
    keys = jnp.concatenate([prompt_all, resp_kv], 0)
    total = keys.shape[0]
    position = jnp.arange(rows, dtype=jnp.int32)
    key_pos = jnp.arange(total, dtype=jnp.int32) - prompt_rows
    allowed = key_pos[None, :] <= position[:, None]
    live = position < length
    q_flat = queries.reshape(rows * heads, width)
    scores = (
        jnp.dot(q_flat, keys.T, preferred_element_type=jnp.float32).reshape(rows, heads, total)
        * softmax_scale
    )
    scores = jnp.where(allowed[:, None, :], scores, masked_value)
    top = jnp.max(scores, axis=-1, keepdims=True)
    expo = jnp.exp(scores - top)
    probs = (expo / jnp.sum(expo, axis=-1, keepdims=True)).reshape(rows * heads, total)
    probs_b = probs.astype(jnp.bfloat16)
    d_flat = jnp.where(live[:, None, None], grad_out, jnp.zeros_like(grad_out)).reshape(
        rows * heads, latent
    )
    values = keys[:, :latent]
    out_vals = jnp.dot(probs_b, values, preferred_element_type=jnp.float32)
    delta = jnp.sum(d_flat.astype(jnp.float32) * out_vals, axis=-1, keepdims=True)
    d_prob = jnp.dot(d_flat, values.T, preferred_element_type=jnp.float32)
    d_score = (softmax_scale * probs * (d_prob - delta)).astype(jnp.bfloat16)
    d_query = (
        jnp.dot(d_score, keys, preferred_element_type=jnp.float32)
        .astype(jnp.bfloat16)
        .reshape(rows, heads, width)
    )
    dims = (((0,), (0,)), ((), ()))
    d_keys = lax.dot_general(d_score, q_flat, dims, preferred_element_type=jnp.float32)
    d_vals = lax.dot_general(probs_b, d_flat, dims, preferred_element_type=jnp.float32)
    d_kv = jnp.concatenate([d_keys[:, :latent] + d_vals, d_keys[:, latent:]], 1)
    return (d_query, d_kv[:prompt_rows], d_kv[prompt_rows:])


def body(queries, grad_out, prompt_kv, resp_kv, lengths):
    prompt_all = lax.all_gather(prompt_kv, "resp", axis=0, tiled=True)
    d_query, prompt_term, resp_term = local_grads(
        queries, grad_out, prompt_all, resp_kv, lengths[0]
    )
    mine = lax.psum_scatter(prompt_term, "resp", scatter_dimension=0, tiled=True)
    prompt_sum, resp_sum = lax.psum((mine, resp_term), "tp")
    grad_prompt = prompt_sum.astype(jnp.bfloat16)
    return (d_query, grad_prompt, resp_sum.astype(jnp.bfloat16))


def solution(mesh):
    return jax.shard_map(
        body,
        mesh=mesh,
        in_specs=(
            P(("grp", "resp"), "tp", None),
            P(("grp", "resp"), "tp", None),
            P(("grp", "resp"), None),
            P(("grp", "resp"), None),
            P(("grp", "resp")),
        ),
        out_specs=(
            P(("grp", "resp"), "tp", None),
            P(("grp", "resp"), None),
            P(("grp", "resp"), None),
        ),
        check_vma=False,
    )
```

profile of v0, /device:TPU:24, one launch (start us, length us, event | category | flops | bytes accessed | tf_op | source)
XLA Modules:
  0.0 270.0 jit_solution(6868184996795718049)
XLA Ops:
  7.2 0.0 copy-start.4
  7.2 0.0 reduce-scatter.4.cloned.1.call-start
  7.9 0.1 iota_compare_fusion
  8.0 0.0 copy-start
  8.0 1.1 copy.21
  9.1 0.4 broadcast_bitcast_fusion
  9.6 2.0 copy.23
  11.5 0.0 copy-done.4
  11.5 42.2 %all_gather.3 = bf16[768,576]{1,0:T(8,128)(2,1)} all-gather(bf16[48,576]{1,0:T(8,128)(2,1)S(1)} %copy-done.4), channel_id=1, replica_groups=mesh['grp'=4,'resp'=16,'tp'=8] {'resp'}, dimensions={0}, use_global_device_ids=true | all-gather | bytes 940032 | tf_op jit(solution)/shard_map/all_gather | solution.py:51
  53.7 0.0 copy-done
  53.7 0.2 select_bitcast_fusion
  53.9 1.3 copy.24
  55.2 2.2 copy.22
  57.4 3.2 %fusion.13 = (f32[1024]{0:T(1024)S(1)}, f32[1024,896]{0,1:T(8,128)S(1)}) fusion(pred[1024,896]{0,1:T(32,128)(4,1)} %copy.23, bf16[128,8,576]{2,1,0:T(8,128)(2,1)S(1)} %copy.22, bf16[128,576]{1,0:T(8,128)(2,1)S(1)} %copy.21, bf16[768,576]{1,0:T(8,128)(2,1)} %all_gather.3), kind=kOutput, calls=%fused_computation.27 | convolution fusion | flops 1061780480 | bytes 6803456 | tf_op jit(solution)/shard_map/dot_general | solution.py:22
  60.7 0.0 copy-start.1
  60.7 0.0 copy-start.2
  60.7 0.5 fusion.1
  61.2 0.7 copy-done.1
  61.9 0.3 copy-done.2
  62.2 1.4 multiply_reduce_fusion
  63.6 1.4 multiply_convert_fusion
  65.0 0.0 copy-start.5
  65.0 1.5 fusion.3
  66.5 0.0 copy-done.5
  66.5 1.4 slice_add_fusion
  67.9 1.4 fusion.2
  69.2 0.0 copy-start.3
  69.2 2.9 %copy.30 = f32[768,576]{1,0:T(8,128)} copy(f32[768,576]{0,1:T(8,128)} %fusion.2) | data formatting | bytes 3538944
  72.1 0.0 reduce-scatter.4.cloned.1.call-update
  72.2 0.0 copy-done.3
  72.2 3.9 %convolution_convert_fusion = bf16[1024,576]{0,1:T(8,128)(2,1)} fusion(bf16[1024,896]{0,1:T(8,128)(2,1)} %copy-done.5, bf16[128,576]{1,0:T(8,128)(2,1)S(1)} %copy.21, bf16[768,576]{1,0:T(8,128)(2,1)S(1)} %copy-done.3), kind=kOutput, calls=%fused_computation.11 | convolution fusion | flops 1059618816 | bytes 4046848 | tf_op jit(solution)/shard_map/dot_general | solution.py:39
  76.1 1.7 copy.26
  77.8 1.8 copy.27
  79.6 98.3 %reduce-scatter.4.cloned.1.call-done = f32[48,576]{1,0:T(8,128)} async-done(((f32[768,576]{1,0:T(8,128)}), f32[48,576]{1,0:T(8,128)}) %reduce-scatter.4.cloned.1.call-update) | async-done | bytes 110608
  178.0 1.0 copy.31
  179.0 83.4 %all-reduce.2 = (bf16[48,576]{0,1:T(8,128)(2,1)S(1)}, bf16[128,576]{0,1:T(8,128)(2,1)}) all-reduce(f32[48,576]{0,1:T(8,128)S(1)} %copy.31, f32[128,576]{0,1:T(8,128)S(1)} %pad_maximum_fusion.6), channel_id=1, replica_groups=mesh['grp'=4,'resp'=16,'tp'=8] {'tp'}, use_global_device_ids=true, to_apply=%region_4.5 | all-reduce | flops 101376 | bytes 608256 | tf_op jit(solution)/shard_map/psum | solution.py:56
  262.4 0.7 copy.28
  (4 shorter events, 0.0 us)
Async XLA Ops:
  7.2 4.4 %copy-start.4 = (bf16[48,576]{1,0:T(8,128)(2,1)S(1)}, bf16[48,576]{1,0:T(8,128)(2,1)}, u32[]{:S(2)}) copy-start(bf16[48,576]{1,0:T(8,128)(2,1)} %param.7) | copy-start | bytes 165892
  7.2 170.8 %reduce-scatter.4.cloned.1.call-start = ((), (), s32[]{:S(2)}) async-start(), calls=%async_computation.1 | async-start | bytes 2088960
  8.0 45.7 %copy-start = (bf16[128,8,512]{2,1,0:T(8,128)(2,1)S(1)}, bf16[128,8,512]{2,1,0:T(8,128)(2,1)}, u32[]{:S(2)}) copy-start(bf16[128,8,512]{2,1,0:T(8,128)(2,1)} %param.6) | copy-start | bytes 3145732
  60.7 1.2 copy-start.1
  60.7 1.5 copy-start.2
  65.0 1.5 copy-start.5
  69.2 2.9 %copy-start.3 = (bf16[768,576]{1,0:T(8,128)(2,1)S(1)}, bf16[768,576]{1,0:T(8,128)(2,1)}, u32[]{:S(2)}) copy-start(bf16[768,576]{1,0:T(8,128)(2,1)} %all_gather.3) | copy-start | bytes 2654212
Sparse Core Ops, SparseCore 0:
  72.3 105.6 reduce-scatter.3
where the time goes:
time: 271 us; the launch traced here: 270 us
  blocking collectives  126 us (46%)
  waiting for transfers between devices  98.4 us (36%)
  local copies, waits for them, and re-layouts  16.2 us (6%)
  between operations  14.8 us (5%)
  matrix products  12.8 us (5%)
    unnamed x2, waiting for transfers between devices  98.4 us
    psum x1, blocking collectives, body(): prompt_sum, resp_sum = lax.psum((mine, resp_term), 'tp')  83.4 us
    all_gather x1, blocking collectives, body(): prompt_all = lax.all_gather(prompt_kv, 'resp', axis=0, tiled=True)  42.2 us
    unnamed x18, local copies, waits for them, and re-layouts  10.8 us
  transfers between devices with their start and end apart: 1, of which 1 were waited for; matrix products, arithmetic and copies ran while one was open for 3% of the time, Pallas kernels for 0%

commit v1 on v0

v1 whole, which is shorter than its diff:
```python
import functools

import jax
import jax.numpy as jnp
from jax import lax
from jax.experimental import pallas as pl
from jax.experimental.pallas import tpu as pltpu
from jax.sharding import Mesh, PartitionSpec as P

softmax_scale = 192 ** (-0.5)
log2_e = 1.4426950408889634
masked_value = -1e30
f32, bf16 = jnp.float32, jnp.bfloat16

LAT, ROPE, WIDTH = 512, 64, 576
BLOCK, PACKED = 48, 56
RESP, RESP_PACKED = 128, 144
GRID = (4, 8, 2, 2, 4)
AXES = ("grp", "zlo", "core", "zhi", "x")

SMEM = pl.BlockSpec(memory_space=pltpu.SMEM)
VMEM = pl.BlockSpec(memory_space=pltpu.VMEM)


def call(kernel, ins, out, scratch=(), limit=16, flops=0):
    moved = sum(o.size * o.dtype.itemsize for o in out)
    many = len(out) > 1
    return pl.pallas_call(
        kernel,
        out_shape=tuple(out) if many else out[0],
        in_specs=ins,
        out_specs=tuple(VMEM for _ in out) if many else VMEM,
        scratch_shapes=list(scratch),
        compiler_params=pltpu.CompilerParams(vmem_limit_bytes=limit * 2**20),
        cost_estimate=pl.CostEstimate(flops=flops, bytes_accessed=2 * moved, transcendentals=0),
    )


def shape(dims, dtype):
    return jax.ShapeDtypeStruct(dims, dtype)


def pack_prompt(x_ref, rows_ref, out_ref):
    x = x_ref[0]
    rows = rows_ref[...].astype(f32)
    lat = rows[:, 0:128]
    rope = rows[0:16, LAT:WIDTH]
    for q in range(1, 4):
        lat = jnp.where(x == q, rows[:, 128 * q : 128 * q + 128], lat)
        if q < 3:
            rope = jnp.where(x == q, rows[16 * q : 16 * q + 16, LAT:WIDTH], rope)
    rope = jnp.concatenate([rope[0:8], rope[8:16]], 1)
    block = jnp.concatenate([lat, rope], 0).astype(bf16)
    for z in range(out_ref.shape[0]):
        out_ref[z] = block


def pack_block(lat, rope, q):
    lat = lat[:, 128 * q : 128 * q + 128].reshape(8, BLOCK, 128)
    if q < 3:
        rope = rope.reshape(8, BLOCK, ROPE)[:, 16 * q : 16 * q + 16]
        rope = jnp.concatenate([rope[:, 0:8], rope[:, 8:16]], 2)
    else:
        rope = jnp.zeros((8, 8, 128), f32)
    return jnp.concatenate([lat, rope], 1)


NT = (((1,), (1,)), ((), ()))


def main_kernel(core_ref, len_ref, prompt_ref, resp_ref, q_ref, d_ref, k_ref, ds_ref, send_ref, keep_ref,
                keep_resp_ref, p_ref):
    core = core_ref[0]
    length = len_ref[0]
    for half in range(2):
        who = core if half == 0 else 1 - core
        at = 384 * half
        rope = []
        for q in range(4):
            got = prompt_ref[who, q]
            k_ref[at : at + 384, 128 * q : 128 * q + 128] = got[:, 0:48].reshape(384, 128)
            if q < 3:
                two = got[:, 48:56].astype(f32)
                rope += [two[:, :, 0:64], two[:, :, 64:128]]
        k_ref[at : at + 384, LAT:WIDTH] = jnp.concatenate(rope, 1).reshape(384, ROPE).astype(bf16)
    k_ref[768:896, :] = resp_ref[...]

    key_at = lax.broadcasted_iota(jnp.int32, (RESP, 256), 0)
    slot = lax.broadcasted_iota(jnp.int32, (RESP, 256), 1) % 128
    allowed = key_at <= slot
    live = lax.broadcasted_iota(jnp.int32, (1, 256), 1) % 128 < length
    for pair in range(4):
        q_pair = jnp.concatenate([q_ref[2 * pair], q_ref[2 * pair + 1]], 1)
        scores = jnp.dot(k_ref[...], q_pair, preferred_element_type=f32) * (softmax_scale * log2_e)
        scores = jnp.concatenate([scores[0:768], jnp.where(allowed, scores[768:896], masked_value)], 0)
        top = jnp.max(scores, axis=0, keepdims=True)
        expo = jnp.exp2(scores - top)
        total = jnp.sum(expo, axis=0, keepdims=True)
        d_pair = d_ref[256 * pair : 256 * pair + 256]
        d_prob = lax.dot_general(k_ref[:, 0:LAT], d_pair, NT, preferred_element_type=f32)
        inverse = 1.0 / total
        delta = jnp.sum(expo * d_prob, axis=0, keepdims=True) * inverse
        probs = expo * jnp.where(live, inverse, 0.0)
        p_ref[:, 256 * pair : 256 * pair + 256] = probs.astype(bf16)
        ds_ref[:, 256 * pair : 256 * pair + 256] = (probs * (d_prob - delta) * softmax_scale).astype(bf16)

    def grads(lo, hi):
        d_lat = jnp.zeros((hi - lo, LAT), f32)
        d_rope = jnp.zeros((hi - lo, ROPE), f32)
        d_lat = jnp.dot(p_ref[lo:hi], d_ref[...], preferred_element_type=f32)
        q_all = jnp.concatenate([q_ref[h] for h in range(8)], 1)
        d_lat = d_lat + lax.dot_general(ds_ref[lo:hi], q_all[0:LAT], NT, preferred_element_type=f32)
        d_rope = lax.dot_general(ds_ref[lo:hi], q_all[LAT:WIDTH], NT, preferred_element_type=f32)
        return d_lat, d_rope

    lat, rope = grads(384, 768)
    for q in range(4):
        send_ref[q] = pack_block(lat, rope, q).astype(bf16)
    lat, rope = grads(0, 384)
    for q in range(4):
        keep_ref[q] = pack_block(lat, rope, q)
    lat, rope = grads(768, 896)
    for q in range(4):
        two = rope[32 * q : 32 * q + 32]
        two = jnp.concatenate([two[0:16], two[16:32]], 1)
        keep_resp_ref[q] = jnp.concatenate([lat[:, 128 * q : 128 * q + 128], two], 0).astype(bf16)


def query_kernel(k_ref, ds_ref, out_ref):
    k_t = k_ref[...].T
    for pair in range(4):
        got = jnp.dot(k_t, ds_ref[:, 256 * pair : 256 * pair + 256], preferred_element_type=f32).astype(bf16)
        out_ref[2 * pair] = got[:, 0:128]
        out_ref[2 * pair + 1] = got[:, 128:256]


def core_sum(core_ref, got_ref, keep_ref, keep_resp_ref, out_ref):
    other = 1 - core_ref[0]
    for q in range(4):
        both = keep_ref[q] + got_ref[other, q].astype(f32)
        out_ref[q, 0:448] = both.reshape(448, 128).astype(bf16)
        out_ref[q, 448:592] = keep_resp_ref[q]


def x_sum(got_ref, prompt_ref, resp_ref):
    total = got_ref[0].astype(f32)
    for q in range(1, 4):
        total = total + got_ref[q].astype(f32)
    total = total.astype(bf16)
    for z in range(8):
        block = total[PACKED * z : PACKED * z + PACKED]
        prompt_ref[2 * z] = block
        prompt_ref[2 * z + 1] = block
    resp_ref[...] = total[448:592]


def last_sum(got_ref, mine_ref, far_ref, out_ref):
    total = got_ref[0].astype(f32)
    for z in range(1, 16):
        total = total + got_ref[z].astype(f32)
    resp = (mine_ref[...].astype(f32) + far_ref[...].astype(f32)).astype(bf16)
    total = total.astype(bf16)
    for q in range(4):
        out_ref[q, 0:RESP_PACKED] = resp
        out_ref[q, RESP_PACKED : RESP_PACKED + PACKED] = total


def unpack(got_ref, prompt_ref, resp_ref):
    resp_rope, prompt_rope = [], []
    for q in range(4):
        got = got_ref[q].astype(f32)
        resp_ref[128 * q : 128 * q + 128, :] = got[0:128].T.astype(bf16)
        resp_rope += [got[128:144, 0:64], got[128:144, 64:128]]
        prompt_ref[:, 128 * q : 128 * q + 128] = got[144:192].astype(bf16)
        if q < 3:
            prompt_rope += [got[192:200, 0:64], got[192:200, 64:128]]
    resp_ref[LAT:WIDTH, :] = jnp.concatenate(resp_rope, 0).T.astype(bf16)
    prompt_ref[:, LAT:WIDTH] = jnp.concatenate(prompt_rope, 0).astype(bf16)


def body(queries, grad_out, prompt_kv, resp_kv, lengths):
    x_at = lax.axis_index("x").astype(jnp.int32).reshape(1)
    core_at = lax.axis_index("core").astype(jnp.int32).reshape(1)
    q_t = jnp.transpose(queries, (1, 2, 0))
    d_heads = jnp.transpose(grad_out, (1, 0, 2)).reshape(8 * RESP, LAT)

    mine = call(pack_prompt, [SMEM, VMEM], [shape((8, PACKED, 128), bf16)])(x_at, prompt_kv)
    along_z = lax.all_to_all(mine, "zlo", 0, 0, tiled=True)
    along_x = lax.all_gather(along_z, "x")
    prompt = lax.all_gather(along_x, "core")

    keys, d_score, send, keep, keep_resp = call(
        main_kernel,
        [SMEM, SMEM, VMEM, VMEM, VMEM, VMEM],
        [
            shape((896, WIDTH), bf16),
            shape((896, 1024), bf16),
            shape((4, 8, PACKED, 128), bf16),
            shape((4, 8, PACKED, 128), f32),
            shape((4, RESP_PACKED, 128), bf16),
        ],
        scratch=[pltpu.VMEM((896, 1024), bf16)],
        limit=40,
        flops=4 * 2 * 1024 * 896 * 576,
    )(core_at, lengths, prompt, resp_kv, q_t, d_heads)

    got = lax.all_gather(send, "core")
    parts = call(core_sum, [SMEM, VMEM, VMEM, VMEM], [shape((4, 592, 128), bf16)])(core_at, got, keep, keep_resp)
    parts = lax.all_to_all(parts, "x", 0, 0, tiled=True)
    d_query = call(
        query_kernel, [VMEM, VMEM], [shape((8, WIDTH, 128), bf16)], limit=24, flops=2 * 1024 * 896 * 576
    )(keys, d_score)
    terms, resp_mine = call(x_sum, [VMEM], [shape((16, PACKED, 128), bf16), shape((RESP_PACKED, 128), bf16)])(parts)
    terms = lax.all_to_all(terms, ("zlo", "zhi"), 0, 0, tiled=True)
    resp_far = lax.ppermute(resp_mine, "zhi", [(0, 1), (1, 0)])
    final = call(last_sum, [VMEM, VMEM, VMEM], [shape((4, 200, 128), bf16)])(terms, resp_mine, resp_far)
    final = lax.all_to_all(final, "x", 0, 0, tiled=True)
    grad_prompt, grad_resp = call(unpack, [VMEM], [shape((BLOCK, WIDTH), bf16), shape((WIDTH, RESP), bf16)])(final)
    return (jnp.transpose(d_query, (2, 0, 1)), grad_prompt, grad_resp.T)


def solution(mesh):
    split = Mesh(mesh.devices.reshape(GRID), AXES)
    rows = ("grp", "zlo", "core")
    heads = ("zhi", "x")
    return jax.shard_map(
        body,
        mesh=split,
        in_specs=(P(rows, heads, None), P(rows, heads, None), P(rows, None), P(rows, None), P(rows)),
        out_specs=(P(rows, heads, None), P(rows, None), P(rows, None)),
        check_vma=False,
    )
```

time: 271 us -> 110 us (0.41)
  blocking collectives: 126 us -> 32.2 us
  waiting for transfers between devices: 98.4 us -> 21.5 us
  starting transfers between devices: 0.04 us -> 36.1 us
  between operations: 14.8 us -> 1.33 us
  matrix products: 12.8 us -> 0 us
  Pallas kernels: 0 us -> 12.3 us
  local copies, waits for them, and re-layouts: 16.2 us -> 5.67 us
    unnamed x2 -> x0, waiting for transfers between devices: 98.4 us -> none
    psum x1 -> x0, blocking collectives: 83.4 us -> none  [body(): prompt_sum, resp_sum = lax.psum((mine, resp_term), 'tp')]
    all_gather x1 -> x3, blocking collectives: 42.2 us -> 18.6 us  [the longest x1 13.7 us: body(): along_x = lax.all_gather(along_z, 'x')]
    all_to_all x0 -> x3, starting transfers between devices: none -> 23.6 us  [the longest x1 12.5 us: body(): along_z = lax.all_to_all(mine, 'zlo', 0, 0, tiled=True)]
    all_to_all x0 -> x1, blocking collectives: none -> 13.6 us  [body(): parts = lax.all_to_all(parts, 'x', 0, 0, tiled=True)]
    dot_general x6 -> x0, matrix products: 12.8 us -> none  [the longest x1 3.95 us: local_grads(): jnp.dot(d_score, keys, preferred_element_type=jnp.float32)]
    ppermute x0 -> x1, starting transfers between devices: none -> 12.5 us  [body(): resp_far = lax.ppermute(resp_mine, 'zhi', [(0, 1), (1, 0)])]
    pallas_call x0 -> x7, Pallas kernels: none -> 12.3 us  [the longest x1 6.73 us: body(): call(main_kernel, [SMEM, SMEM, VMEM, VMEM, VMEM, VMEM], [shape((896, WIDT...]
  transfers between devices with their start and end apart: 1 -> 4, of which waited for: 1 -> 3; matrix products, arithmetic and copies ran while one was open for 3% -> 3% of each run, Pallas kernels for 0% -> 2%
where the time goes in v1:
time: 110 us; the launch traced here: 109 us
  starting transfers between devices  36.1 us (33%)
  blocking collectives  32.2 us (29%)
  waiting for transfers between devices  21.5 us (20%)
  Pallas kernels  12.3 us (11%)
  local copies, waits for them, and re-layouts  5.67 us (5%)
  between operations  1.33 us (1%)
    all_gather x1, blocking collectives, body(): along_x = lax.all_gather(along_z, 'x')  13.7 us
    all_to_all x1, blocking collectives, body(): parts = lax.all_to_all(parts, 'x', 0, 0, tiled=True)  13.6 us
    ppermute x1, starting transfers between devices, body(): resp_far = lax.ppermute(resp_mine, 'zhi', [(0, 1), (1, 0)])  12.5 us
    all_to_all x1, starting transfers between devices, body(): along_z = lax.all_to_all(mine, 'zlo', 0, 0, tiled=True)  12.5 us
    ppermute x1, waiting for transfers between devices, body(): resp_far = lax.ppermute(resp_mine, 'zhi', [(0, 1), (1, 0)])  10.3 us
    all_to_all x1, starting transfers between devices, body(): terms = lax.all_to_all(terms, ('zlo', 'zhi'), 0, 0, tiled=True)  7.69 us
    all_to_all x1, waiting for transfers between devices, body(): along_z = lax.all_to_all(mine, 'zlo', 0, 0, tiled=True)  7.34 us
    pallas_call x1, Pallas kernels, body(): call(main_kernel, [SMEM, SMEM, VMEM, VMEM, VMEM, VMEM], [shape((896, WIDT...  6.73 us
  transfers between devices with their start and end apart: 4, of which 3 were waited for; matrix products, arithmetic and copies ran while one was open for 3% of the time, Pallas kernels for 2%

profile of v1, /device:TPU:24, one launch (start us, length us, event | category | flops | bytes accessed | tf_op | source)
XLA Modules:
  0.0 109.1 jit_solution(11867756283907553621)
XLA Ops:
  0.6 0.0 copy-start.1
  0.6 0.8 copy-done.1
  1.5 0.7 shard_map.76
  2.2 12.5 %all-to-all-start = ((bf16[8,56,128]{2,1,0:T(8,128)(2,1)}), bf16[8,56,128]{2,1,0:T(8,128)(2,1)S(1)}, u32[]{:S(2)}, u32[]{:S(2)}) async-start(bf16[8,56,128]{2,1,0:T(8,128)(2,1)} %shard_map.76), calls=%async_computation | async-start | bytes 229376 | tf_op jit(solution)/shard_map/all_to_all | solution.py:188
  15.4 1.1 copy.11.resp_ref
  16.4 2.5 %copy.10 = bf16[8,128,512]{2,1,0:T(8,128)(2,1)} copy(bf16[8,128,512]{2,0,1:T(8,128)(2,1)} %bitcast.16) | data formatting | bytes 2097152 | tf_op jit(solution)/shard_map/transpose | solution.py:185
  18.9 7.3 %all-to-all-done = bf16[8,56,128]{2,1,0:T(8,128)(2,1)S(1)} async-done(((bf16[8,56,128]{2,1,0:T(8,128)(2,1)}), bf16[8,56,128]{2,1,0:T(8,128)(2,1)S(1)}, u32[]{:S(2)}, u32[]{:S(2)}) %all-to-all-start) | async-done | bytes 114720 | tf_op jit(solution)/shard_map/all_to_all | solution.py:188
  26.3 0.0 copy-start
  26.3 13.7 %all-gather = bf16[32,56,128]{2,1,0:T(8,128)(2,1)S(1)} all-gather(bf16[8,56,128]{2,1,0:T(8,128)(2,1)S(1)} %all-to-all-done), channel_id=2, replica_groups=mesh['grp'=4,'zlo'=8,'core'=2,'zhi'=2,'x'=4] {'x'}, dimensions={0}, use_global_device_ids=true | all-gather | bytes 573440 | tf_op jit(solution)/shard_map/all_gather | solution.py:189
  39.9 2.5 %all-gather.1 = bf16[8,8,56,128]{3,2,1,0:T(8,128)(2,1)S(1)} all-gather(bf16[4,8,56,128]{3,2,1,0:T(8,128)(2,1)S(1)} %bitcast.14), channel_id=3, replica_groups=mesh['grp'=4,'zlo'=8,'core'=2,'zhi'=2,'x'=4] {'core'}, dimensions={0}, use_global_device_ids=true | all-gather | bytes 1376256 | tf_op jit(solution)/shard_map/all_gather | solution.py:190
  42.4 0.0 copy-done
  42.4 0.0 copy-start.2
  42.4 1.3 %copy-done.2 = bf16[128,8,576]{0,2,1:T(8,128)(2,1)S(1)} copy-done((bf16[128,8,576]{0,2,1:T(8,128)(2,1)S(1)}, bf16[128,8,576]{0,2,1:T(8,128)(2,1)}, u32[]{:S(2)}) %copy-start.2) | copy-done | bytes 1179672
  43.7 6.7 %shard_map.77 = (bf16[896,576]{1,0:T(8,128)(2,1)S(1)}, bf16[896,1024]{1,0:T(8,128)(2,1)S(1)}, bf16[4,8,56,128]{3,2,1,0:T(8,128)(2,1)S(1)}, f32[4,8,56,128]{3,2,1,0:T(8,128)S(1)}, bf16[4,144,128]{2,1,0:T(8,128)(2,1)S(1)}) custom-call(s32[1]{0:T(128)} %bitcast.core_ref, s32[1]{0:T(128)S(6)} %copy.12.len_ref, bf16[2,4,8,56,128]{4,3,2,1,0:T(8,128)(2,1)S(1)} %bitcast.12, ...), custom_call_target="tpu_custom_call" | custom-call | flops 4227858432 | bytes 8781824 | tf_op jit(solution)/shard_map/pallas_call | solution.py:192
  50.4 2.5 %all-gather.2 = bf16[8,8,56,128]{3,2,1,0:T(8,128)(2,1)S(1)} all-gather(bf16[4,8,56,128]{3,2,1,0:T(8,128)(2,1)S(1)} %get-tuple-element.14), channel_id=4, replica_groups=mesh['grp'=4,'zlo'=8,'core'=2,'zhi'=2,'x'=4] {'core'}, dimensions={0}, use_global_device_ids=true | all-gather | bytes 1376256 | tf_op jit(solution)/shard_map/all_gather | solution.py:207
  52.9 0.1 shard_map.79
  52.9 13.6 %all_to_all.20.got_ref = bf16[4,592,128]{2,1,0:T(8,128)(2,1)S(1)} all-to-all(bf16[4,592,128]{2,1,0:T(8,128)(2,1)S(1)} %shard_map.79), channel_id=1, replica_groups=mesh['grp'=4,'zlo'=8,'core'=2,'zhi'=2,'x'=4] {'x'}, dimensions={0} | all-to-all | bytes 1212416 | tf_op jit(solution)/shard_map/all_to_all | solution.py:209
  66.5 0.8 shard_map.80
  67.3 7.7 %all-to-all-start.2 = ((bf16[16,56,128]{2,1,0:T(8,128)(2,1)}), bf16[16,56,128]{2,1,0:T(8,128)(2,1)S(1)}, u32[]{:S(2)}, u32[]{:S(2)}) async-start(bf16[16,56,128]{2,1,0:T(8,128)(2,1)} %get-tuple-element.17), calls=%async_computation.2 | async-start | bytes 458752 | tf_op jit(solution)/shard_map/all_to_all | solution.py:214
  75.0 12.5 %collective-permute-start = (bf16[144,128]{1,0:T(8,128)(2,1)S(1)}, bf16[144,128]{1,0:T(8,128)(2,1)S(1)}, u32[]{:S(2)}, u32[]{:S(2)}) collective-permute-start(bf16[144,128]{1,0:T(8,128)(2,1)S(1)} %get-tuple-element.18.mine_ref), channel_id=1, source_target_pairs={{0,4},{4,0},{1,5},{5,1},{2,6},{6,2},{3,7},{7,3},{8,12},{12,8},{9,1... | collective-permute-start | bytes 110600 | tf_op jit(solution)/shard_map/ppermute | solution.py:215
  87.5 10.3 %collective-permute-done.far_ref = bf16[144,128]{1,0:T(8,128)(2,1)S(1)} collective-permute-done((bf16[144,128]{1,0:T(8,128)(2,1)S(1)}, bf16[144,128]{1,0:T(8,128)(2,1)S(1)}, u32[]{:S(2)}, u32[]{:S(2)}) %collective-permute-start) | collective-permute-done | bytes 36896 | tf_op jit(solution)/shard_map/ppermute | solution.py:215
  97.8 0.0 all-to-all-done.2.got_ref
  97.8 0.7 shard_map.81
  98.6 3.4 %all-to-all-start.3 = ((bf16[4,200,128]{2,1,0:T(8,128)(2,1)}), bf16[4,200,128]{2,1,0:T(8,128)(2,1)S(1)}, u32[]{:S(2)}, u32[]{:S(2)}) async-start(bf16[4,200,128]{2,1,0:T(8,128)(2,1)} %shard_map.81), calls=%async_computation.3 | async-start | bytes 409600 | tf_op jit(solution)/shard_map/all_to_all | solution.py:217
  101.9 2.4 %shard_map.78 = bf16[8,576,128]{2,1,0:T(8,128)(2,1)} custom-call(bf16[896,576]{1,0:T(8,128)(2,1)S(1)} %get-tuple-element.12.k_ref, bf16[896,1024]{1,0:T(8,128)(2,1)S(1)} %get-tuple-element.13.ds_ref), custom_call_target="tpu_custom_call" | custom-call | flops 1056964608 | bytes 2359296 | tf_op jit(solution)/shard_map/pallas_call | solution.py:210
  104.4 3.9 %all-to-all-done.3.got_ref = bf16[4,200,128]{2,1,0:T(8,128)(2,1)S(1)} async-done(((bf16[4,200,128]{2,1,0:T(8,128)(2,1)}), bf16[4,200,128]{2,1,0:T(8,128)(2,1)S(1)}, u32[]{:S(2)}, u32[]{:S(2)}) %all-to-all-start.3) | async-done | bytes 204832 | tf_op jit(solution)/shard_map/all_to_all | solution.py:217
  108.3 0.9 shard_map.82
Async XLA Ops:
  0.6 0.8 copy-start.1
  2.2 24.1 %all-to-all-start = ((bf16[8,56,128]{2,1,0:T(8,128)(2,1)}), bf16[8,56,128]{2,1,0:T(8,128)(2,1)S(1)}, u32[]{:S(2)}, u32[]{:S(2)}) async-start(bf16[8,56,128]{2,1,0:T(8,128)(2,1)} %shard_map.76), calls=%async_computation | async-start | bytes 229376 | tf_op jit(solution)/shard_map/all_to_all | solution.py:188
  26.3 16.1 %copy-start = (bf16[8,128,512]{2,1,0:T(8,128)(2,1)S(1)}, bf16[8,128,512]{2,1,0:T(8,128)(2,1)}, u32[]{:S(2)}) copy-start(bf16[8,128,512]{2,1,0:T(8,128)(2,1)} %copy.10) | copy-start | bytes 3145732
  42.4 1.3 %copy-start.2 = (bf16[128,8,576]{0,2,1:T(8,128)(2,1)S(1)}, bf16[128,8,576]{0,2,1:T(8,128)(2,1)}, u32[]{:S(2)}) copy-start(bf16[128,8,576]{0,2,1:T(8,128)(2,1)} %param.5) | copy-start | bytes 3538948
  67.3 30.5 %all-to-all-start.2 = ((bf16[16,56,128]{2,1,0:T(8,128)(2,1)}), bf16[16,56,128]{2,1,0:T(8,128)(2,1)S(1)}, u32[]{:S(2)}, u32[]{:S(2)}) async-start(bf16[16,56,128]{2,1,0:T(8,128)(2,1)} %get-tuple-element.17), calls=%async_computation.2 | async-start | bytes 458752 | tf_op jit(solution)/shard_map/all_to_all | solution.py:214
  75.0 22.8 %collective-permute-start = (bf16[144,128]{1,0:T(8,128)(2,1)S(1)}, bf16[144,128]{1,0:T(8,128)(2,1)S(1)}, u32[]{:S(2)}, u32[]{:S(2)}) collective-permute-start(bf16[144,128]{1,0:T(8,128)(2,1)S(1)} %get-tuple-element.18.mine_ref), channel_id=1, source_target_pairs={{0,4},{4,0},{1,5},{5,1},{2,6},{6,2},{3,7},{7,3},{8,12},{12,8},{9,1... | collective-permute-start | bytes 110600 | tf_op jit(solution)/shard_map/ppermute | solution.py:215
  98.6 9.7 %all-to-all-start.3 = ((bf16[4,200,128]{2,1,0:T(8,128)(2,1)}), bf16[4,200,128]{2,1,0:T(8,128)(2,1)S(1)}, u32[]{:S(2)}, u32[]{:S(2)}) async-start(bf16[4,200,128]{2,1,0:T(8,128)(2,1)} %shard_map.81), calls=%async_computation.3 | async-start | bytes 409600 | tf_op jit(solution)/shard_map/all_to_all | solution.py:217

commit v2 on v1

--- a/solution.py
+++ b/solution.py
@@ -20,6 +20,7 @@
 
 SMEM = pl.BlockSpec(memory_space=pltpu.SMEM)
 VMEM = pl.BlockSpec(memory_space=pltpu.VMEM)
+HBM = pl.BlockSpec(memory_space=pl.ANY)
 
 
 def call(kernel, ins, out, scratch=(), limit=16, flops=0):
@@ -63,6 +64,12 @@
     else:
         rope = jnp.zeros((8, 8, 128), f32)
     return jnp.concatenate([lat, rope], 1)
+
+
+def bring_near(far_ref, near_ref, sem):
+    copy = pltpu.make_async_copy(far_ref, near_ref, sem)
+    copy.start()
+    copy.wait()
 
 
 NT = (((1,), (1,)), ((), ()))
@@ -105,8 +112,6 @@
         ds_ref[:, 256 * pair : 256 * pair + 256] = (probs * (d_prob - delta) * softmax_scale).astype(bf16)
 
     def grads(lo, hi):
-        d_lat = jnp.zeros((hi - lo, LAT), f32)
-        d_rope = jnp.zeros((hi - lo, ROPE), f32)
         d_lat = jnp.dot(p_ref[lo:hi], d_ref[...], preferred_element_type=f32)
         q_all = jnp.concatenate([q_ref[h] for h in range(8)], 1)
         d_lat = d_lat + lax.dot_general(ds_ref[lo:hi], q_all[0:LAT], NT, preferred_element_type=f32)
@@ -184,9 +189,11 @@
     q_t = jnp.transpose(queries, (1, 2, 0))
     d_heads = jnp.transpose(grad_out, (1, 0, 2)).reshape(8 * RESP, LAT)
 
+    q_t = call(bring_near, [HBM], [shape((8, WIDTH, 128), bf16)], scratch=[pltpu.SemaphoreType.DMA])(q_t)
     mine = call(pack_prompt, [SMEM, VMEM], [shape((8, PACKED, 128), bf16)])(x_at, prompt_kv)
     along_z = lax.all_to_all(mine, "zlo", 0, 0, tiled=True)
-    along_x = lax.all_gather(along_z, "x")
+    along_x = jnp.broadcast_to(along_z[None], (4, 8, PACKED, 128))
+    along_x = lax.all_to_all(along_x, "x", 0, 0, tiled=True)
     prompt = lax.all_gather(along_x, "core")
 
     keys, d_score, send, keep, keep_resp = call(

time: 110 us -> 107 us (0.973)
  blocking collectives: 32.2 us -> 42.4 us
  starting transfers between devices: 36.1 us -> 27.9 us
  local copies, waits for them, and re-layouts: 5.67 us -> 3.13 us
  waiting for transfers between devices: 21.5 us -> 19.6 us
    all_to_all x0 -> x1, blocking collectives: none -> 24 us  [body(): along_z = lax.all_to_all(mine, 'zlo', 0, 0, tiled=True)]
    all_gather x1 -> x0, blocking collectives: 13.7 us -> none  [body(): along_x = lax.all_gather(along_z, 'x')]
    all_to_all x1, starting transfers between devices: 12.5 us -> 4.29 us  [body(): along_x = lax.all_to_all(along_x, 'x', 0, 0, tiled=True)]
    unnamed x7 -> x15, local copies, waits for them, and re-layouts: 3.16 us -> 1.01 us
    all_to_all x1, waiting for transfers between devices: 7.34 us -> 5.35 us  [body(): along_x = lax.all_to_all(along_x, 'x', 0, 0, tiled=True)]
    transpose x1, local copies, waits for them, and re-layouts: 2.51 us -> 1.28 us  [body(): d_heads = jnp.transpose(grad_out, (1, 0, 2)).reshape(8 * RESP, LAT)]
  transfers between devices with their start and end apart: 4 -> 4, of which waited for: 3 -> 3; matrix products, arithmetic and copies ran while one was open for 3% -> 1% of each run, Pallas kernels for 2% -> 3%
where the time goes in v2:
time: 107 us; the launch traced here: 106 us
  blocking collectives  42.4 us (40%)
  starting transfers between devices  27.9 us (26%)
  waiting for transfers between devices  19.6 us (18%)
  Pallas kernels  11.9 us (11%)
  local copies, waits for them, and re-layouts  3.13 us (3%)
  between operations  1.39 us (1%)
    all_to_all x1, blocking collectives, body(): along_z = lax.all_to_all(mine, 'zlo', 0, 0, tiled=True)  24 us
    all_to_all x1, blocking collectives, body(): parts = lax.all_to_all(parts, 'x', 0, 0, tiled=True)  13.3 us
    ppermute x1, starting transfers between devices, body(): resp_far = lax.ppermute(resp_mine, 'zhi', [(0, 1), (1, 0)])  12.5 us
    ppermute x1, waiting for transfers between devices, body(): resp_far = lax.ppermute(resp_mine, 'zhi', [(0, 1), (1, 0)])  10.4 us
    all_to_all x1, starting transfers between devices, body(): terms = lax.all_to_all(terms, ('zlo', 'zhi'), 0, 0, tiled=True)  7.68 us
    pallas_call x1, Pallas kernels, body(): call(main_kernel, [SMEM, SMEM, VMEM, VMEM, VMEM, VMEM], [shape((896, WIDT...  6.7 us
    all_to_all x1, waiting for transfers between devices, body(): along_x = lax.all_to_all(along_x, 'x', 0, 0, tiled=True)  5.35 us
    all_to_all x1, starting transfers between devices, body(): along_x = lax.all_to_all(along_x, 'x', 0, 0, tiled=True)  4.29 us
  transfers between devices with their start and end apart: 4, of which 3 were waited for; matrix products, arithmetic and copies ran while one was open for 1% of the time, Pallas kernels for 3%

profile of v2, /device:TPU:24, one launch (start us, length us, event | category | flops | bytes accessed | tf_op | source)
XLA Modules:
  0.0 106.3 jit_solution(12313774134000098833)
XLA Ops:
  0.6 0.0 copy-start.4
  0.6 0.8 copy-done.4
  1.5 0.0 copy-start.6
  1.5 0.0 copy-start.5
  1.5 0.1 shard_map.76
  1.5 24.0 %all_to_all.25 = bf16[8,56,128]{2,1,0:T(8,128)(2,1)S(1)} all-to-all(bf16[8,56,128]{2,1,0:T(8,128)(2,1)S(1)} %shard_map.76), channel_id=1, replica_groups=mesh['grp'=4,'zlo'=8,'core'=2,'zhi'=2,'x'=4] {'zlo'}, dimensions={0} | all-to-all | bytes 229376 | tf_op jit(solution)/shard_map/all_to_all | solution.py:194
  25.6 0.8 broadcast_in_dim.2
  26.4 4.3 %all-to-all-start.1 = ((bf16[4,8,56,128]{3,2,1,0:T(8,128)(2,1)}), bf16[4,8,56,128]{3,2,1,0:T(8,128)(2,1)S(1)}, u32[]{:S(2)}, u32[]{:S(2)}) async-start(bf16[4,8,56,128]{3,2,1,0:T(8,128)(2,1)} %broadcast_in_dim.2), calls=%async_computation.1 | async-start | bytes 917504 | tf_op jit(solution)/shard_map/all_to_all | solution.py:196
  31.3 0.0 copy-done.6
  31.4 0.0 copy-start
  31.4 0.2 copy.11.resp_ref
  31.5 0.0 copy-done.5
  31.5 1.3 %copy.10 = bf16[8,128,512]{2,1,0:T(8,128)(2,1)} copy(bf16[8,128,512]{2,0,1:T(8,128)(2,1)S(1)} %bitcast.14) | data formatting | bytes 2097152 | tf_op jit(solution)/shard_map/transpose | solution.py:190
  32.8 0.0 copy-done
  32.8 0.2 shard_map.77.q_ref
  33.1 5.3 %all-to-all-done.1 = bf16[4,8,56,128]{3,2,1,0:T(8,128)(2,1)S(1)} async-done(((bf16[4,8,56,128]{3,2,1,0:T(8,128)(2,1)}), bf16[4,8,56,128]{3,2,1,0:T(8,128)(2,1)S(1)}, u32[]{:S(2)}, u32[]{:S(2)}) %all-to-all-start.1) | async-done | bytes 458784 | tf_op jit(solution)/shard_map/all_to_all | solution.py:196
  38.4 0.0 copy-start.3
  38.4 2.6 %all-gather = bf16[8,8,56,128]{3,2,1,0:T(8,128)(2,1)S(1)} all-gather(bf16[4,8,56,128]{3,2,1,0:T(8,128)(2,1)S(1)} %all-to-all-done.1), channel_id=2, replica_groups=mesh['grp'=4,'zlo'=8,'core'=2,'zhi'=2,'x'=4] {'core'}, dimensions={0}, use_global_device_ids=true | all-gather | bytes 1376256 | tf_op jit(solution)/shard_map/all_gather | solution.py:197
  41.0 0.0 copy-done.3
  41.0 6.7 %shard_map.78 = (bf16[896,576]{1,0:T(8,128)(2,1)S(1)}, bf16[896,1024]{1,0:T(8,128)(2,1)S(1)}, bf16[4,8,56,128]{3,2,1,0:T(8,128)(2,1)S(1)}, f32[4,8,56,128]{3,2,1,0:T(8,128)S(1)}, bf16[4,144,128]{2,1,0:T(8,128)(2,1)S(1)}) custom-call(s32[1]{0:T(128)} %bitcast.core_ref, s32[1]{0:T(128)S(6)} %copy.12.len_ref, bf16[2,4,8,56,128]{4,3,2,1,0:T(8,128)(2,1)S(1)} %bitcast.12, ...), custom_call_target="tpu_custom_call" | custom-call | flops 4227858432 | bytes 8781824 | tf_op jit(solution)/shard_map/pallas_call | solution.py:199
  47.7 0.0 copy-start.1
  47.7 2.5 %all-gather.1 = bf16[8,8,56,128]{3,2,1,0:T(8,128)(2,1)S(1)} all-gather(bf16[4,8,56,128]{3,2,1,0:T(8,128)(2,1)S(1)} %get-tuple-element.14), channel_id=3, replica_groups=mesh['grp'=4,'zlo'=8,'core'=2,'zhi'=2,'x'=4] {'core'}, dimensions={0}, use_global_device_ids=true | all-gather | bytes 1376256 | tf_op jit(solution)/shard_map/all_gather | solution.py:214
  50.2 0.1 shard_map.80
  50.3 0.0 copy-done.1
  50.3 13.3 %all_to_all.26.got_ref = bf16[4,592,128]{2,1,0:T(8,128)(2,1)S(1)} all-to-all(bf16[4,592,128]{2,1,0:T(8,128)(2,1)S(1)} %shard_map.80), channel_id=1, replica_groups=mesh['grp'=4,'zlo'=8,'core'=2,'zhi'=2,'x'=4] {'x'}, dimensions={0} | all-to-all | bytes 1212416 | tf_op jit(solution)/shard_map/all_to_all | solution.py:216
  63.6 0.0 copy-start.2
  63.6 0.8 shard_map.81
  64.4 7.7 %all-to-all-start.3 = ((bf16[16,56,128]{2,1,0:T(8,128)(2,1)}), bf16[16,56,128]{2,1,0:T(8,128)(2,1)S(1)}, u32[]{:S(2)}, u32[]{:S(2)}) async-start(bf16[16,56,128]{2,1,0:T(8,128)(2,1)} %get-tuple-element.17), calls=%async_computation.3 | async-start | bytes 458752 | tf_op jit(solution)/shard_map/all_to_all | solution.py:221
  72.1 12.5 %collective-permute-start = (bf16[144,128]{1,0:T(8,128)(2,1)S(1)}, bf16[144,128]{1,0:T(8,128)(2,1)S(1)}, u32[]{:S(2)}, u32[]{:S(2)}) collective-permute-start(bf16[144,128]{1,0:T(8,128)(2,1)S(1)} %get-tuple-element.18.mine_ref), channel_id=1, source_target_pairs={{0,4},{4,0},{1,5},{5,1},{2,6},{6,2},{3,7},{7,3},{8,12},{12,8},{9,1... | collective-permute-start | bytes 110600 | tf_op jit(solution)/shard_map/ppermute | solution.py:222
  84.6 10.4 %collective-permute-done.far_ref = bf16[144,128]{1,0:T(8,128)(2,1)S(1)} collective-permute-done((bf16[144,128]{1,0:T(8,128)(2,1)S(1)}, bf16[144,128]{1,0:T(8,128)(2,1)S(1)}, u32[]{:S(2)}, u32[]{:S(2)}) %collective-permute-start) | collective-permute-done | bytes 36896 | tf_op jit(solution)/shard_map/ppermute | solution.py:222
  95.0 0.0 all-to-all-done.3.got_ref
  95.0 0.7 shard_map.82
  95.7 3.4 %all-to-all-start.4 = ((bf16[4,200,128]{2,1,0:T(8,128)(2,1)}), bf16[4,200,128]{2,1,0:T(8,128)(2,1)S(1)}, u32[]{:S(2)}, u32[]{:S(2)}) async-start(bf16[4,200,128]{2,1,0:T(8,128)(2,1)} %shard_map.82), calls=%async_computation.4 | async-start | bytes 409600 | tf_op jit(solution)/shard_map/all_to_all | solution.py:224
  99.1 0.0 copy-done.2
  99.1 2.4 %shard_map.79 = bf16[8,576,128]{2,1,0:T(8,128)(2,1)} custom-call(bf16[896,576]{1,0:T(8,128)(2,1)S(1)} %copy-done.2, bf16[896,1024]{1,0:T(8,128)(2,1)S(1)} %get-tuple-element.13.ds_ref), custom_call_target="tpu_custom_call" | custom-call | flops 1056964608 | bytes 2359296 | tf_op jit(solution)/shard_map/pallas_call | solution.py:217
  101.5 3.9 %all-to-all-done.4.got_ref = bf16[4,200,128]{2,1,0:T(8,128)(2,1)S(1)} async-done(((bf16[4,200,128]{2,1,0:T(8,128)(2,1)}), bf16[4,200,128]{2,1,0:T(8,128)(2,1)S(1)}, u32[]{:S(2)}, u32[]{:S(2)}) %all-to-all-start.4) | async-done | bytes 204832 | tf_op jit(solution)/shard_map/all_to_all | solution.py:224
  105.4 0.9 shard_map.83
Async XLA Ops:
  0.6 0.8 copy-start.4
  1.5 29.9 %copy-start.6 = (bf16[128,576]{0,1:T(8,128)(2,1)S(1)}, bf16[128,576]{0,1:T(8,128)(2,1)}, u32[]{:S(2)}) copy-start(bf16[128,576]{0,1:T(8,128)(2,1)} %param.8) | copy-start | bytes 442372
  1.5 30.1 %copy-start.5 = (bf16[128,8,512]{2,1,0:T(8,128)(2,1)S(1)}, bf16[128,8,512]{2,1,0:T(8,128)(2,1)}, u32[]{:S(2)}) copy-start(bf16[128,8,512]{2,1,0:T(8,128)(2,1)} %param.6) | copy-start | bytes 3145732
  26.4 12.0 %all-to-all-start.1 = ((bf16[4,8,56,128]{3,2,1,0:T(8,128)(2,1)}), bf16[4,8,56,128]{3,2,1,0:T(8,128)(2,1)S(1)}, u32[]{:S(2)}, u32[]{:S(2)}) async-start(bf16[4,8,56,128]{3,2,1,0:T(8,128)(2,1)} %broadcast_in_dim.2), calls=%async_computation.1 | async-start | bytes 917504 | tf_op jit(solution)/shard_map/all_to_all | solution.py:196
  31.4 1.5 %copy-start = (bf16[128,8,576]{0,2,1:T(8,128)(2,1)S(1)}, bf16[128,8,576]{0,2,1:T(8,128)(2,1)}, u32[]{:S(2)}) copy-start(bf16[128,8,576]{0,2,1:T(8,128)(2,1)} %param.5) | copy-start | bytes 3538948
  38.4 2.6 %copy-start.3 = (bf16[8,128,512]{2,1,0:T(8,128)(2,1)S(1)}, bf16[8,128,512]{2,1,0:T(8,128)(2,1)}, u32[]{:S(2)}) copy-start(bf16[8,128,512]{2,1,0:T(8,128)(2,1)} %copy.10) | copy-start | bytes 3145732
  47.7 2.6 %copy-start.1 = (bf16[896,576]{1,0:T(8,128)(2,1)}, bf16[896,576]{1,0:T(8,128)(2,1)S(1)}, u32[]{:S(2)}) copy-start(bf16[896,576]{1,0:T(8,128)(2,1)S(1)} %get-tuple-element.12.k_ref) | copy-start | bytes 3096580
  63.6 35.5 %copy-start.2 = (bf16[896,576]{1,0:T(8,128)(2,1)S(1)}, bf16[896,576]{1,0:T(8,128)(2,1)}, u32[]{:S(2)}) copy-start(bf16[896,576]{1,0:T(8,128)(2,1)} %copy-done.1) | copy-start | bytes 3096580
  64.4 30.6 %all-to-all-start.3 = ((bf16[16,56,128]{2,1,0:T(8,128)(2,1)}), bf16[16,56,128]{2,1,0:T(8,128)(2,1)S(1)}, u32[]{:S(2)}, u32[]{:S(2)}) async-start(bf16[16,56,128]{2,1,0:T(8,128)(2,1)} %get-tuple-element.17), calls=%async_computation.3 | async-start | bytes 458752 | tf_op jit(solution)/shard_map/all_to_all | solution.py:221
  72.1 22.9 %collective-permute-start = (bf16[144,128]{1,0:T(8,128)(2,1)S(1)}, bf16[144,128]{1,0:T(8,128)(2,1)S(1)}, u32[]{:S(2)}, u32[]{:S(2)}) collective-permute-start(bf16[144,128]{1,0:T(8,128)(2,1)S(1)} %get-tuple-element.18.mine_ref), channel_id=1, source_target_pairs={{0,4},{4,0},{1,5},{5,1},{2,6},{6,2},{3,7},{7,3},{8,12},{12,8},{9,1... | collective-permute-start | bytes 110600 | tf_op jit(solution)/shard_map/ppermute | solution.py:222
  95.7 9.7 %all-to-all-start.4 = ((bf16[4,200,128]{2,1,0:T(8,128)(2,1)}), bf16[4,200,128]{2,1,0:T(8,128)(2,1)S(1)}, u32[]{:S(2)}, u32[]{:S(2)}) async-start(bf16[4,200,128]{2,1,0:T(8,128)(2,1)} %shard_map.82), calls=%async_computation.4 | async-start | bytes 409600 | tf_op jit(solution)/shard_map/all_to_all | solution.py:224

commit v3 on v2

--- a/solution.py
+++ b/solution.py
@@ -21,6 +21,9 @@
 SMEM = pl.BlockSpec(memory_space=pltpu.SMEM)
 VMEM = pl.BlockSpec(memory_space=pltpu.VMEM)
 HBM = pl.BlockSpec(memory_space=pl.ANY)
+
+
+SCR = [pltpu.VMEM((896, 1024), bf16), pltpu.VMEM((2, 896, 256), f32), pltpu.VMEM((2, 896, 256), f32)]
 
 
 def call(kernel, ins, out, scratch=(), limit=16, flops=0):
@@ -76,7 +79,7 @@
 
 
 def main_kernel(core_ref, len_ref, prompt_ref, resp_ref, q_ref, d_ref, k_ref, ds_ref, send_ref, keep_ref,
-                keep_resp_ref, p_ref):
+                keep_resp_ref, p_ref, s_ref, dp_ref):
     core = core_ref[0]
     length = len_ref[0]
     for half in range(2):
@@ -96,20 +99,44 @@
     slot = lax.broadcasted_iota(jnp.int32, (RESP, 256), 1) % 128
     allowed = key_at <= slot
     live = lax.broadcasted_iota(jnp.int32, (1, 256), 1) % 128 < length
-    for pair in range(4):
+    def products(pair):
         q_pair = jnp.concatenate([q_ref[2 * pair], q_ref[2 * pair + 1]], 1)
-        scores = jnp.dot(k_ref[...], q_pair, preferred_element_type=f32) * (softmax_scale * log2_e)
-        scores = jnp.concatenate([scores[0:768], jnp.where(allowed, scores[768:896], masked_value)], 0)
-        top = jnp.max(scores, axis=0, keepdims=True)
-        expo = jnp.exp2(scores - top)
-        total = jnp.sum(expo, axis=0, keepdims=True)
+        scores = jnp.dot(k_ref[...], q_pair, preferred_element_type=f32)
         d_pair = d_ref[256 * pair : 256 * pair + 256]
         d_prob = lax.dot_general(k_ref[:, 0:LAT], d_pair, NT, preferred_element_type=f32)
-        inverse = 1.0 / total
-        delta = jnp.sum(expo * d_prob, axis=0, keepdims=True) * inverse
-        probs = expo * jnp.where(live, inverse, 0.0)
-        p_ref[:, 256 * pair : 256 * pair + 256] = probs.astype(bf16)
-        ds_ref[:, 256 * pair : 256 * pair + 256] = (probs * (d_prob - delta) * softmax_scale).astype(bf16)
+        s_ref[pair % 2] = scores
+        dp_ref[pair % 2] = d_prob
+
+    def weights(pair):
+        at = pair % 2
+        tops = [s_ref[at, 128 * i : 128 * i + 128].reshape(16, 8, 256).max(0) for i in range(6)]
+        last = jnp.where(allowed, s_ref[at, 768:896], masked_value)
+        s_ref[at, 768:896] = last
+        tops.append(last.reshape(16, 8, 256).max(0))
+        top = functools.reduce(jnp.maximum, tops).max(0, keepdims=True)
+        total = jnp.zeros((8, 256), f32)
+        weighed = jnp.zeros((8, 256), f32)
+        for i in range(7):
+            rows = slice(128 * i, 128 * i + 128)
+            expo = jnp.exp2((s_ref[at, rows] - top) * (softmax_scale * log2_e))
+            s_ref[at, rows] = expo
+            total = total + expo.reshape(16, 8, 256).sum(0)
+            weighed = weighed + (expo * dp_ref[at, rows]).reshape(16, 8, 256).sum(0)
+        inverse = 1.0 / total.sum(0, keepdims=True)
+        delta = weighed.sum(0, keepdims=True) * inverse
+        share = jnp.where(live, inverse, 0.0)
+        scaled = share * softmax_scale
+        for i in range(7):
+            rows = slice(128 * i, 128 * i + 128)
+            expo = s_ref[at, rows]
+            p_ref[rows, 256 * pair : 256 * pair + 256] = (expo * share).astype(bf16)
+            ds_ref[rows, 256 * pair : 256 * pair + 256] = (expo * scaled * (dp_ref[at, rows] - delta)).astype(bf16)
+
+    products(0)
+    for pair in range(4):
+        if pair < 3:
+            products(pair + 1)
+        weights(pair)
 
     def grads(lo, hi):
         d_lat = jnp.dot(p_ref[lo:hi], d_ref[...], preferred_element_type=f32)
@@ -154,8 +181,8 @@
     total = total.astype(bf16)
     for z in range(8):
         block = total[PACKED * z : PACKED * z + PACKED]
-        prompt_ref[2 * z] = block
-        prompt_ref[2 * z + 1] = block
+        prompt_ref[z] = block
+        prompt_ref[z + 8] = block
     resp_ref[...] = total[448:592]
 
 
@@ -174,7 +201,7 @@
     resp_rope, prompt_rope = [], []
     for q in range(4):
         got = got_ref[q].astype(f32)
-        resp_ref[128 * q : 128 * q + 128, :] = got[0:128].T.astype(bf16)
+        resp_ref[128 * q : 128 * q + 128, :] = got_ref[q, 0:128].T
         resp_rope += [got[128:144, 0:64], got[128:144, 64:128]]
         prompt_ref[:, 128 * q : 128 * q + 128] = got[144:192].astype(bf16)
         if q < 3:
@@ -206,7 +233,7 @@
             shape((4, 8, PACKED, 128), f32),
             shape((4, RESP_PACKED, 128), bf16),
         ],
-        scratch=[pltpu.VMEM((896, 1024), bf16)],
+        scratch=SCR,
         limit=40,
         flops=4 * 2 * 1024 * 896 * 576,
     )(core_at, lengths, prompt, resp_kv, q_t, d_heads)
@@ -218,8 +245,9 @@
         query_kernel, [VMEM, VMEM], [shape((8, WIDTH, 128), bf16)], limit=24, flops=2 * 1024 * 896 * 576
     )(keys, d_score)
     terms, resp_mine = call(x_sum, [VMEM], [shape((16, PACKED, 128), bf16), shape((RESP_PACKED, 128), bf16)])(parts)
-    terms = lax.all_to_all(terms, ("zlo", "zhi"), 0, 0, tiled=True)
+    terms = lax.all_to_all(terms, ("zhi", "zlo"), 0, 0, tiled=True)
     resp_far = lax.ppermute(resp_mine, "zhi", [(0, 1), (1, 0)])
+    resp_far, d_query = lax.optimization_barrier((resp_far, d_query))
     final = call(last_sum, [VMEM, VMEM, VMEM], [shape((4, 200, 128), bf16)])(terms, resp_mine, resp_far)
     final = lax.all_to_all(final, "x", 0, 0, tiled=True)
     grad_prompt, grad_resp = call(unpack, [VMEM], [shape((BLOCK, WIDTH), bf16), shape((WIDTH, RESP), bf16)])(final)

time: 107 us -> 105 us (0.981)
  blocking collectives: 42.4 us -> 51.1 us
  waiting for transfers between devices: 19.6 us -> 12.1 us
  starting transfers between devices: 27.9 us -> 24.5 us
  local copies, waits for them, and re-layouts: 3.13 us -> 4.37 us
  Pallas kernels: 11.9 us -> 10.7 us
    all_to_all x0 -> x1, blocking collectives: none -> 8.74 us  [body(): final = lax.all_to_all(final, 'x', 0, 0, tiled=True)]
    all_to_all x2 -> x1, waiting for transfers between devices: 3.9 us -> 0.01 us  [body(): terms = lax.all_to_all(terms, ('zhi', 'zlo'), 0, 0, tiled=True)]
    ppermute x1, waiting for transfers between devices: 10.4 us -> 6.77 us  [body(): resp_far = lax.ppermute(resp_mine, 'zhi', [(0, 1), (1, 0)])]
    all_to_all x2 -> x1, starting transfers between devices: 11.1 us -> 7.69 us  [body(): terms = lax.all_to_all(terms, ('zhi', 'zlo'), 0, 0, tiled=True)]
    unnamed x15, local copies, waits for them, and re-layouts: 1.01 us -> 2.26 us
  transfers between devices with their start and end apart: 4 -> 3, of which waited for: 3 -> 2; matrix products, arithmetic and copies ran while one was open for 1% -> 1% of each run, Pallas kernels for 3% -> 3%
where the time goes in v3:
time: 105 us; the launch traced here: 104 us
  blocking collectives  51.1 us (49%)
  starting transfers between devices  24.5 us (23%)
  waiting for transfers between devices  12.1 us (12%)
  Pallas kernels  10.7 us (10%)
  local copies, waits for them, and re-layouts  4.37 us (4%)
  between operations  1.38 us (1%)
    all_to_all x1, blocking collectives, body(): along_z = lax.all_to_all(mine, 'zlo', 0, 0, tiled=True)  24 us
    all_to_all x1, blocking collectives, body(): parts = lax.all_to_all(parts, 'x', 0, 0, tiled=True)  13.3 us
    ppermute x1, starting transfers between devices, body(): resp_far = lax.ppermute(resp_mine, 'zhi', [(0, 1), (1, 0)])  12.5 us
    all_to_all x1, blocking collectives, body(): final = lax.all_to_all(final, 'x', 0, 0, tiled=True)  8.74 us
    all_to_all x1, starting transfers between devices, body(): terms = lax.all_to_all(terms, ('zhi', 'zlo'), 0, 0, tiled=True)  7.69 us
    ppermute x1, waiting for transfers between devices, body(): resp_far = lax.ppermute(resp_mine, 'zhi', [(0, 1), (1, 0)])  6.77 us
    pallas_call x1, Pallas kernels, body(): call(main_kernel, [SMEM, SMEM, VMEM, VMEM, VMEM, VMEM], [shape((896, WIDT...  6.22 us
    all_to_all x1, waiting for transfers between devices, body(): along_x = lax.all_to_all(along_x, 'x', 0, 0, tiled=True)  5.35 us
  transfers between devices with their start and end apart: 3, of which 2 were waited for; matrix products, arithmetic and copies ran while one was open for 1% of the time, Pallas kernels for 3%

profile of v3, /device:TPU:24, one launch (start us, length us, event | category | flops | bytes accessed | tf_op | source)
XLA Modules:
  0.0 104.2 jit_solution(15938916779163848652)
XLA Ops:
  0.6 0.0 copy-start.4
  0.6 0.8 copy-done.4
  1.5 0.0 copy-start.6
  1.5 0.0 copy-start.5
  1.5 0.1 shard_map.76
  1.5 24.0 %all_to_all.25 = bf16[8,56,128]{2,1,0:T(8,128)(2,1)S(1)} all-to-all(bf16[8,56,128]{2,1,0:T(8,128)(2,1)S(1)} %shard_map.76), channel_id=1, replica_groups=mesh['grp'=4,'zlo'=8,'core'=2,'zhi'=2,'x'=4] {'zlo'}, dimensions={0} | all-to-all | bytes 229376 | tf_op jit(solution)/shard_map/all_to_all | solution.py:221
  25.6 0.8 broadcast_in_dim.2
  26.4 4.3 %all-to-all-start.1 = ((bf16[4,8,56,128]{3,2,1,0:T(8,128)(2,1)}), bf16[4,8,56,128]{3,2,1,0:T(8,128)(2,1)S(1)}, u32[]{:S(2)}, u32[]{:S(2)}) async-start(bf16[4,8,56,128]{3,2,1,0:T(8,128)(2,1)} %broadcast_in_dim.2), calls=%async_computation.1 | async-start | bytes 917504 | tf_op jit(solution)/shard_map/all_to_all | solution.py:223
  31.3 0.0 copy-done.6
  31.3 0.0 copy-start
  31.4 0.2 copy.11.resp_ref
  31.5 0.0 copy-done.5
  31.5 1.3 %copy.10 = bf16[8,128,512]{2,1,0:T(8,128)(2,1)} copy(bf16[8,128,512]{2,0,1:T(8,128)(2,1)S(1)} %bitcast.14) | data formatting | bytes 2097152 | tf_op jit(solution)/shard_map/transpose | solution.py:217
  32.8 0.0 copy-done
  32.8 0.2 shard_map.77.q_ref
  33.1 5.3 %all-to-all-done.1 = bf16[4,8,56,128]{3,2,1,0:T(8,128)(2,1)S(1)} async-done(((bf16[4,8,56,128]{3,2,1,0:T(8,128)(2,1)}), bf16[4,8,56,128]{3,2,1,0:T(8,128)(2,1)S(1)}, u32[]{:S(2)}, u32[]{:S(2)}) %all-to-all-start.1) | async-done | bytes 458784 | tf_op jit(solution)/shard_map/all_to_all | solution.py:223
  38.4 0.0 copy-start.3
  38.4 2.6 %all-gather = bf16[8,8,56,128]{3,2,1,0:T(8,128)(2,1)S(1)} all-gather(bf16[4,8,56,128]{3,2,1,0:T(8,128)(2,1)S(1)} %all-to-all-done.1), channel_id=2, replica_groups=mesh['grp'=4,'zlo'=8,'core'=2,'zhi'=2,'x'=4] {'core'}, dimensions={0}, use_global_device_ids=true | all-gather | bytes 1376256 | tf_op jit(solution)/shard_map/all_gather | solution.py:224
  41.0 0.0 copy-done.3
  41.0 6.2 %shard_map.78 = (bf16[896,576]{1,0:T(8,128)(2,1)S(1)}, bf16[896,1024]{1,0:T(8,128)(2,1)S(1)}, bf16[4,8,56,128]{3,2,1,0:T(8,128)(2,1)S(1)}, f32[4,8,56,128]{3,2,1,0:T(8,128)S(1)}, bf16[4,144,128]{2,1,0:T(8,128)(2,1)S(1)}) custom-call(s32[1]{0:T(128)} %bitcast.core_ref, s32[1]{0:T(128)S(6)} %copy.12.len_ref, bf16[2,4,8,56,128]{4,3,2,1,0:T(8,128)(2,1)S(1)} %bitcast.12, ...), custom_call_target="tpu_custom_call" | custom-call | flops 4227858432 | bytes 8781824 | tf_op jit(solution)/shard_map/pallas_call | solution.py:226
  47.2 0.0 copy-start.1
  47.2 2.5 %all-gather.1 = bf16[8,8,56,128]{3,2,1,0:T(8,128)(2,1)S(1)} all-gather(bf16[4,8,56,128]{3,2,1,0:T(8,128)(2,1)S(1)} %get-tuple-element.14), channel_id=3, replica_groups=mesh['grp'=4,'zlo'=8,'core'=2,'zhi'=2,'x'=4] {'core'}, dimensions={0}, use_global_device_ids=true | all-gather | bytes 1376256 | tf_op jit(solution)/shard_map/all_gather | solution.py:241
  49.7 0.1 shard_map.79
  49.8 0.0 copy-done.1
  49.8 13.3 %all_to_all.26.got_ref = bf16[4,592,128]{2,1,0:T(8,128)(2,1)S(1)} all-to-all(bf16[4,592,128]{2,1,0:T(8,128)(2,1)S(1)} %shard_map.79), channel_id=1, replica_groups=mesh['grp'=4,'zlo'=8,'core'=2,'zhi'=2,'x'=4] {'x'}, dimensions={0} | all-to-all | bytes 1212416 | tf_op jit(solution)/shard_map/all_to_all | solution.py:243
  63.1 0.7 shard_map.80
  63.9 7.7 %all-to-all-start.3 = ((bf16[16,56,128]{2,1,0:T(8,128)(2,1)}), bf16[16,56,128]{2,1,0:T(8,128)(2,1)S(1)}, u32[]{:S(2)}, u32[]{:S(2)}) async-start(bf16[16,56,128]{2,1,0:T(8,128)(2,1)} %get-tuple-element.21), calls=%async_computation.3 | async-start | bytes 458752 | tf_op jit(solution)/shard_map/all_to_all | solution.py:248
  71.6 12.5 %collective-permute-start = (bf16[144,128]{1,0:T(8,128)(2,1)S(1)}, bf16[144,128]{1,0:T(8,128)(2,1)S(1)}, u32[]{:S(2)}, u32[]{:S(2)}) collective-permute-start(bf16[144,128]{1,0:T(8,128)(2,1)S(1)} %get-tuple-element.17.mine_ref), channel_id=1, source_target_pairs={{0,4},{4,0},{1,5},{5,1},{2,6},{6,2},{3,7},{7,3},{8,12},{12,8},{9,1... | collective-permute-start | bytes 110600 | tf_op jit(solution)/shard_map/ppermute | solution.py:249
  84.1 0.0 copy-start.2
  84.1 1.2 %copy-done.2 = bf16[896,576]{1,0:T(8,128)(2,1)S(1)} copy-done((bf16[896,576]{1,0:T(8,128)(2,1)S(1)}, bf16[896,576]{1,0:T(8,128)(2,1)}, u32[]{:S(2)}) %copy-start.2) | copy-done | bytes 1032216
  85.4 2.4 %shard_map.81 = bf16[8,576,128]{2,1,0:T(8,128)(2,1)} custom-call(bf16[896,576]{1,0:T(8,128)(2,1)S(1)} %copy-done.2, bf16[896,1024]{1,0:T(8,128)(2,1)S(1)} %get-tuple-element.19.ds_ref), custom_call_target="tpu_custom_call" | custom-call | flops 1056964608 | bytes 2359296 | tf_op jit(solution)/shard_map/pallas_call | solution.py:244
  87.8 6.8 %collective-permute-done.far_ref = bf16[144,128]{1,0:T(8,128)(2,1)S(1)} collective-permute-done((bf16[144,128]{1,0:T(8,128)(2,1)S(1)}, bf16[144,128]{1,0:T(8,128)(2,1)S(1)}, u32[]{:S(2)}, u32[]{:S(2)}) %collective-permute-start) | collective-permute-done | bytes 36896 | tf_op jit(solution)/shard_map/ppermute | solution.py:249
  94.6 0.0 all-to-all-done.3.got_ref
  94.6 0.1 shard_map.82
  94.6 8.7 %all_to_all.27.got_ref = bf16[4,200,128]{2,1,0:T(8,128)(2,1)S(1)} all-to-all(bf16[4,200,128]{2,1,0:T(8,128)(2,1)S(1)} %shard_map.82), channel_id=1, replica_groups=mesh['grp'=4,'zlo'=8,'core'=2,'zhi'=2,'x'=4] {'x'}, dimensions={0} | all-to-all | bytes 409600 | tf_op jit(solution)/shard_map/all_to_all | solution.py:252
  103.4 0.8 shard_map.83
Async XLA Ops:
  0.6 0.8 copy-start.4
  1.5 29.9 %copy-start.6 = (bf16[128,576]{0,1:T(8,128)(2,1)S(1)}, bf16[128,576]{0,1:T(8,128)(2,1)}, u32[]{:S(2)}) copy-start(bf16[128,576]{0,1:T(8,128)(2,1)} %param.8) | copy-start | bytes 442372
  1.5 30.1 %copy-start.5 = (bf16[128,8,512]{2,1,0:T(8,128)(2,1)S(1)}, bf16[128,8,512]{2,1,0:T(8,128)(2,1)}, u32[]{:S(2)}) copy-start(bf16[128,8,512]{2,1,0:T(8,128)(2,1)} %param.6) | copy-start | bytes 3145732
  26.4 12.0 %all-to-all-start.1 = ((bf16[4,8,56,128]{3,2,1,0:T(8,128)(2,1)}), bf16[4,8,56,128]{3,2,1,0:T(8,128)(2,1)S(1)}, u32[]{:S(2)}, u32[]{:S(2)}) async-start(bf16[4,8,56,128]{3,2,1,0:T(8,128)(2,1)} %broadcast_in_dim.2), calls=%async_computation.1 | async-start | bytes 917504 | tf_op jit(solution)/shard_map/all_to_all | solution.py:223
  31.3 1.5 %copy-start = (bf16[128,8,576]{0,2,1:T(8,128)(2,1)S(1)}, bf16[128,8,576]{0,2,1:T(8,128)(2,1)}, u32[]{:S(2)}) copy-start(bf16[128,8,576]{0,2,1:T(8,128)(2,1)} %param.5) | copy-start | bytes 3538948
  38.4 2.6 %copy-start.3 = (bf16[8,128,512]{2,1,0:T(8,128)(2,1)S(1)}, bf16[8,128,512]{2,1,0:T(8,128)(2,1)}, u32[]{:S(2)}) copy-start(bf16[8,128,512]{2,1,0:T(8,128)(2,1)} %copy.10) | copy-start | bytes 3145732
  47.2 2.6 %copy-start.1 = (bf16[896,576]{1,0:T(8,128)(2,1)}, bf16[896,576]{1,0:T(8,128)(2,1)S(1)}, u32[]{:S(2)}) copy-start(bf16[896,576]{1,0:T(8,128)(2,1)S(1)} %get-tuple-element.18.k_ref) | copy-start | bytes 3096580
  63.9 30.7 %all-to-all-start.3 = ((bf16[16,56,128]{2,1,0:T(8,128)(2,1)}), bf16[16,56,128]{2,1,0:T(8,128)(2,1)S(1)}, u32[]{:S(2)}, u32[]{:S(2)}) async-start(bf16[16,56,128]{2,1,0:T(8,128)(2,1)} %get-tuple-element.21), calls=%async_computation.3 | async-start | bytes 458752 | tf_op jit(solution)/shard_map/all_to_all | solution.py:248
  71.6 23.0 %collective-permute-start = (bf16[144,128]{1,0:T(8,128)(2,1)S(1)}, bf16[144,128]{1,0:T(8,128)(2,1)S(1)}, u32[]{:S(2)}, u32[]{:S(2)}) collective-permute-start(bf16[144,128]{1,0:T(8,128)(2,1)S(1)} %get-tuple-element.17.mine_ref), channel_id=1, source_target_pairs={{0,4},{4,0},{1,5},{5,1},{2,6},{6,2},{3,7},{7,3},{8,12},{12,8},{9,1... | collective-permute-start | bytes 110600 | tf_op jit(solution)/shard_map/ppermute | solution.py:249
  84.1 1.3 %copy-start.2 = (bf16[896,576]{1,0:T(8,128)(2,1)S(1)}, bf16[896,576]{1,0:T(8,128)(2,1)}, u32[]{:S(2)}) copy-start(bf16[896,576]{1,0:T(8,128)(2,1)} %copy-done.1) | copy-start | bytes 3096580
